TPU v7x, 256 devices: a whole 4x4x8 slice. The times are simulated.
256 devices in a mesh: tunnel: 32 (over x_hi, z, core), cross: 8 (over x_lo, y).
Axes of the slice: x: 4 (x_hi: 2, x_lo: 2; x = x_hi * 2 + x_lo), y: 4, z: 8, core: 2. Of those that a mesh axis runs over, the one named last changes fastest.
Arguments:
- smoke_air_quantities: float32 [5, 64, 64, 4096], P(None, 'cross', None, 'tunnel'), may hold values from -6 to 6
- lining_state: float32 [3, 16, 256, 4096], P(None, None, 'cross', 'tunnel'), may hold values from -6 to 6
- velocity: float32 [64, 64, 4096], P('cross', None, 'tunnel'), may hold values from 0.1 to 0.5
- diffusion: float32 [5], replicated, may hold values from 0.02 to 0.08
- yields: float32 [5], replicated, may hold values from 0.3 to 3
- rates: float32 [8], replicated, may hold values from 0.05 to 0.15
- fire_cells: int32 [256], replicated, may hold values from 0 to 16777215
- release: float32 [256], replicated, may hold values from 0.5 to 5
- face_cells: int32 [20480], P(('tunnel', 'cross')), may hold values from 0 to 511, as said below
- face_cycle: int32 [20480], P(('tunnel', 'cross')), may hold values from 0 to 255, as said below
- face_count: int32 [256], P(('tunnel', 'cross')), may hold values from 14 to 80, as said below
Outputs:
- fire_out: float32 [5, 64, 64, 4096], P(None, 'cross', None, 'tunnel')
- lining_out: float32 [3, 16, 256, 4096], P(None, None, 'cross', 'tunnel')
Inputs may be any that keep to these rules, and one draw needn't show every extreme that they name: `face_cells`: in each device's block of 80 slots the first face_count entries are the cells h * 64 + w of the device's own height band that touch a side wall, the floor or the roof (a corner cell twice); later slots hold 0. `face_cycle`: cycle cell touched by each face row, in the row's own axial segment. Floor, right wall, roof and left wall follow one another round the cycle, turned by an offset that is the same for all segments. Within one axial segment no two live rows name the same cycle cell. Later slots hold 0. `face_count`: devices whose band has the floor or the roof carry more rows than middle bands.
All inputs are finite; a program needn't handle non-finite values.
Results may differ from a plain program's by a relative error of at most 0.00002.
Values sent between devices are 32-bit elements; how exact they have to be, the bound alone decides.
A program may use at most 128 MiB of HBM per device.

v0:
```python
import jax
import jax.numpy as jnp
from jax import lax
from jax.experimental import pallas as pl
from jax.experimental.pallas import tpu as pltpu
from jax.sharding import PartitionSpec as P

SUBSTEPS = 4
NF = 5
CH = 8
BW = 64
SEG = 128
LD = 16
ARC = 32
NBLK = 3 * LD
NT = 32
NC = 8
ROWS = 80
FIELD_SIGN = (1.0, 1.0, -1.0, 1.0, 1.0)
ORDER = (2, 1, 3, 4, 0)
F32 = jnp.float32
BF16 = jnp.bfloat16


def iota(shape, dim):
    return lax.broadcasted_iota(jnp.int32, shape, dim)


def dot_nt(a, b):
    return lax.dot_general(a, b, (((1,), (1,)), ((), ())), preferred_element_type=F32)


def pick(table, rows):
    a = rows.astype(BF16)
    rest = rows - a.astype(F32)
    b = rest.astype(BF16)
    d = (rest - b.astype(F32)).astype(BF16)
    parts = jnp.concatenate([a, b, d], axis=1)
    out = lax.dot_general(table, parts, (((1,), (0,)), ((), ())), preferred_element_type=F32)
    n = rows.shape[1]
    return out[:, 0:n] + out[:, n:2 * n] + out[:, 2 * n:3 * n]


def kernel(
    gas, lin, vel, dif_in, yld_in, rat_in, fcell_in, frel_in, fcl_in, fcy_in, fcn_in,
    out_gas, out_lin,
    S, L, V, FS, WM, GP, GL, GR, LP, LL, LR, CU, CD, HD, HU, TL, TB, CM, CT, NM, HM, PT, NK,
    MSK, TLP, TLR, TGC, TGP, TGQ, TGM, TGE, E, EL, SE, dif, yld, rat, fcn, fcell, frel, fcl, fcy,
    ys, yr, xs, xr, cs, cr, ls, lr, tls, tlr, tgs, tgr, tbs, tbr, loc,
):
    t = lax.axis_index("tunnel")
    c = lax.axis_index("cross")
    not_bottom = c > 0
    not_top = c < NC - 1
    not_first = t > 0
    not_last = t < NT - 1
    is_end = (c == 0) | (c == NC - 1)
    up = (t, (c + 1) % NC)
    down = (t, (c + NC - 1) % NC)
    right = (t + 1, c)
    left = (t - 1, c)
    peers = [(c + k) % NC for k in range(1, NC)]
    origins = [(c + NC - k) % NC for k in range(1, NC)]
    edge_row = jnp.where(c == NC - 1, CH, 1)
    lane = iota((8, SEG), 1)
    pair = lane // 2
    odd = lane % 2 == 1
    lane64 = iota((BW, SEG), 1)
    lane32 = iota((ARC, SEG), 1)

    def remote(src, dst, ssem, rsem, dev):
        return pltpu.make_async_remote_copy(
            src_ref=src, dst_ref=dst, send_sem=ssem, recv_sem=rsem,
            device_id=dev, device_id_type=pl.DeviceIdType.MESH,
        )

    mid = pl.ds(8, BW)

    def y_up(s, f):
        return remote(S.at[s, f, CH, mid], S.at[s, f, 0, mid], ys.at[s, f, 0], yr.at[s, f, 0], up)

    def y_down(s, f):
        return remote(S.at[s, f, 1, mid], S.at[s, f, CH + 1, mid], ys.at[s, f, 1], yr.at[s, f, 1], down)

    def y_first(f, row, side, dev):
        dst = S.at[0, f, (CH + 1) * side, mid]
        return remote(gas.at[f, row], dst, ys.at[0, f, side], yr.at[0, f, side], dev)

    def x_right(s, f):
        return remote(GP.at[s, f], GL.at[s, f], xs.at[s, f, 0], xr.at[s, f, 0], right)

    def x_left(s, f):
        return remote(GP.at[s, f], GR.at[s, f], xs.at[s, f, 1], xr.at[s, f, 1], left)

    def c_up(s):
        return remote(CU.at[s], HD.at[s], cs.at[s, 0], cr.at[s, 0], up)

    def c_down(s):
        return remote(CD.at[s], HU.at[s], cs.at[s, 1], cr.at[s, 1], down)

    def l_right(s):
        return remote(LP.at[s], LL.at[s], ls.at[s, 0], lr.at[s, 0], right)

    def l_left(s):
        return remote(LP.at[s], LR.at[s], ls.at[s, 1], lr.at[s, 1], left)

    def at_rim(b):
        return (b == 0) | (b == NC - 1)

    def arc_of(b):
        return pl.ds(pl.multiple_of(b * ARC, ARC), ARC)

    def eight_of(b):
        return pl.ds(pl.multiple_of(b * 8, 8), 8)

    def tl_whole(s, k):
        part = TL.at[s, arc_of(c)]
        return remote(part, part, tls.at[s, k], tlr.at[s, k], (t, peers[k]))

    def tl_first(k):
        return remote(lin.at[0], TL.at[0, arc_of(c)], tls.at[0, k], tlr.at[0, k], (t, peers[k]))

    def tl_placed(s, k):
        return remote(
            TLP.at[s, eight_of(peers[k])], TLR.at[s, eight_of(c)], tls.at[s, k], tlr.at[s, k], (t, peers[k])
        )

    def tg_mid(s, k):
        return remote(
            TGP.at[s, eight_of(peers[k])], TGM.at[s, eight_of(c)], tgs.at[s, k], tgr.at[s, k], (t, peers[k])
        )

    def tg_rim(s, k):
        return remote(
            TGQ.at[s, arc_of(peers[k])], TGE.at[s, c // (NC - 1)], tgs.at[s, k], tgr.at[s, k], (t, peers[k])
        )

    def tb_all(k):
        return remote(TB.at[c], TB.at[c], tbs.at[k], tbr.at[k], (t, peers[k]))

    def guarded(cond, copy, act):
        @pl.when(cond)
        def _():
            getattr(copy(), act)()

    def y_pair(s, f, act):
        guarded(not_top if act != "wait_recv" else not_bottom, lambda: y_up(s, f), act)
        guarded(not_bottom if act != "wait_recv" else not_top, lambda: y_down(s, f), act)

    def x_pair(s, f, act):
        guarded(not_last if act != "wait_recv" else not_first, lambda: x_right(s, f), act)
        guarded(not_first if act != "wait_recv" else not_last, lambda: x_left(s, f), act)

    def c_pair(s, act):
        getattr(c_up(s), act)()
        getattr(c_down(s), act)()

    def l_pair(s, act):
        guarded(not_last if act != "wait_recv" else not_first, lambda: l_right(s), act)
        guarded(not_first if act != "wait_recv" else not_last, lambda: l_left(s), act)

    def either(cond, one, two, act):
        guarded(cond, one, act)
        guarded(jnp.logical_not(cond), two, act)

    def tl_group(s, act):
        for k in range(NC - 1):
            whole = is_end if act == "wait_recv" else at_rim(peers[k])
            either(whole | (s == 0), lambda: tl_whole(s, k), lambda: tl_placed(s, k), act)

    def tg_group(s, act):
        for k in range(NC - 1):
            rim = at_rim(origins[k]) if act == "wait_recv" else is_end
            either(rim, lambda: tg_rim(s, k), lambda: tg_mid(s, k), act)

    def tb_group(act):
        for k in range(NC - 1):
            getattr(tb_all(k), act)()

    def load_gas(f):
        return pltpu.make_async_copy(gas.at[f], S.at[0, f, pl.ds(1, CH), mid], loc.at[f])

    def load_lin():
        return pltpu.make_async_copy(lin, L.at[0, :, pl.ds(8, ARC)], loc.at[5])

    def load_vel():
        return pltpu.make_async_copy(vel, V, loc.at[6])

    barrier = pltpu.get_barrier_semaphore()

    def greet(dev):
        pl.semaphore_signal(barrier, inc=1, device_id=dev, device_id_type=pl.DeviceIdType.MESH)

    for b in peers:
        greet((t, b))
    pl.when(not_last)(lambda: greet(right))
    pl.when(not_first)(lambda: greet(left))

    small = [
        pltpu.make_async_copy(src, dst, loc.at[7 + i])
        for i, (src, dst) in enumerate(
            ((fcn_in, fcn), (fcl_in, fcl), (fcy_in, fcy), (fcell_in, fcell), (frel_in, frel),
             (dif_in, dif), (yld_in, yld), (rat_in, rat))
        )
    ]
    for copy in small:
        copy.start()
    for f in ORDER:
        load_gas(f).start()
    load_lin().start()
    load_vel().start()

    zero_rows = jnp.zeros((8, SEG), F32)
    zero_band = jnp.zeros((BW, SEG), F32)

    def open_band(packed, dst):
        for h in range(CH):
            for wg in range(8):
                dst[h, 8 * wg:8 * wg + 8, :] = pltpu.roll(packed, 127 - 2 * (8 * wg + h), 1)

    def pack_band(s, f):
        acc = zero_rows
        for h in range(CH):
            for wg in range(8):
                idx = 8 * wg + h
                rows = S[s, f, h + 1, 8 + 8 * wg:16 + 8 * wg, :]
                acc = jnp.where(pair == idx, pltpu.roll(rows, 2 * idx + 1, 1), acc)
        GP[s, f] = acc

    def open_arc(packed, f):
        for i in range(LD):
            for g in range(4):
                EL[f * LD + i, 8 * g:8 * g + 8, :] = pltpu.roll(packed, 127 - 2 * (4 * i + g), 1)

    def pack_arc(s, f):
        acc = zero_rows
        for i in range(LD):
            for g in range(4):
                idx = 4 * i + g
                rows = L[s, f * LD + i, 8 + 8 * g:16 + 8 * g, :]
                acc = jnp.where(pair == idx, pltpu.roll(rows, 2 * idx + 1, 1), acc)
        LP[s, f] = acc

    def lining_margins(s):
        for b in range(NBLK):
            CD[s, b:b + 1, :] = L[s, b, 8:9, :]
            CU[s, b:b + 1, :] = L[s, b, 39:40, :]

    def own_surface(s):
        TL[s, arc_of(c), :] = L[s, 0, pl.ds(8, ARC), :]

    def own_walls(s):
        for h in range(CH):
            TGC[h:h + 1, :] = S[s, 0, h + 1, 8:9, :]
            TGC[CH + h:CH + h + 1, :] = S[s, 0, h + 1, 71:72, :]

        @pl.when(is_end)
        def _():
            TGC[16:ROWS, :] = S[s, 0, edge_row, mid, :]
            TGQ[s] = pick(CT[...], TGC[...])
            TGE[s, c // (NC - 1)] = TGQ[s, arc_of(c), :]

        @pl.when(jnp.logical_not(is_end))
        def _():
            for b in range(NC):
                TGP[s, 8 * b:8 * b + 8, :] = MSK[b, 0:8] * TGC[0:8, :] + MSK[b, 8:16] * TGC[8:16, :]
            TGM[s, eight_of(c), :] = TGP[s, eight_of(c), :]

    @pl.loop(0, SUBSTEPS)
    def _(s):
        @pl.loop(0, NF)
        def _(f):
            @pl.loop(1, CH + 1)
            def _(h):
                S[s, f, h, 0:8, :] = zero_rows
                S[s, f, h, 72:80, :] = zero_rows

            @pl.when(c == 0)
            def _():
                S[s, f, 0, mid, :] = zero_band

            @pl.when(c == NC - 1)
            def _():
                S[s, f, CH + 1, mid, :] = zero_band

            @pl.when(t == 0)
            def _():
                GL[s, f] = zero_rows

            @pl.when(t == NT - 1)
            def _():
                GR[s, f] = zero_rows

        @pl.loop(0, 3)
        def _(f):
            @pl.when(t == 0)
            def _():
                LL[s, f] = zero_rows

            @pl.when(t == NT - 1)
            def _():
                LR[s, f] = zero_rows

        TGM[s, 0:8, :] = zero_rows
        TGM[s, 56:64, :] = zero_rows

    @pl.loop(0, CH)
    def _(h):
        WM[h] = zero_band

    pl.semaphore_wait(
        barrier,
        NC - 1 + jnp.where(not_last, 1, 0) + jnp.where(not_first, 1, 0),
    )

    for f in ORDER:
        guarded(not_top, lambda: y_first(f, CH - 1, 0, up), "start")
        guarded(not_bottom, lambda: y_first(f, 0, 1, down), "start")
    for k in range(NC - 1):
        tl_first(k).start()
    for f in ORDER:
        load_gas(f).wait()
        pack_band(0, f)
        x_pair(0, f, "start")
    for copy in small:
        copy.wait()

    live = iota((1, ROWS), 1) < fcn[0]
    TB[c] = jnp.full((8, SEG), -1.0, F32)
    TB[c, 0:1, 0:ROWS] = jnp.where(live, fcl[...], -1).astype(F32)
    TB[c, 1:2, 0:ROWS] = jnp.where(live, fcy[...], -1).astype(F32)
    tb_group("start")
    def side_cell(r):
        return jnp.where(r < CH, r * BW, (r - CH) * BW + BW - 1)

    def edge_cell(h, w):
        return jnp.where((w > 0) & (w < BW - 1), h * BW + w, -2)

    slot = iota((ROWS, SEG), 0)
    own_cell = jnp.where(
        slot < 16,
        side_cell(slot),
        jnp.where(is_end, edge_cell(edge_row - 1, slot - 16), -2),
    ).astype(F32)
    rows_of = (own_cell == TB[c, 0:1, :]).astype(F32)
    cycle_of = (iota((256, SEG), 0).astype(F32) == TB[c, 1:2, :]).astype(BF16)
    seen_by = dot_nt(rows_of.astype(BF16), cycle_of)
    CM[...] = seen_by.astype(BF16)

    @pl.when(is_end)
    def _():
        CT[...] = dot_nt(cycle_of, rows_of.astype(BF16)).astype(BF16)

    seat = jnp.sum(rows_of[0:16] * TB[c, 1:2, :], axis=1, keepdims=True)
    taken = jnp.sum(rows_of[0:16], axis=1, keepdims=True) > 0.0
    for b in range(NC):
        here = taken & (seat >= b * ARC) & (seat < (b + 1) * ARC)
        MSK[b] = jnp.broadcast_to(here.astype(F32), (16, SEG))
    NM[...] = jnp.broadcast_to(jnp.sum(rows_of, axis=1, keepdims=True), (ROWS, SEG))

    own_walls(0)
    tg_group(0, "start")


    load_lin().wait()
    lining_margins(0)
    c_pair(0, "start")
    for f in range(3):
        pack_arc(0, f)
    l_pair(0, "start")
    own_surface(0)

    cells = fcell[...]
    hw = cells // 4096 - c * (CH * BW)
    ax = cells % 4096 - t * SEG
    rel = frel[...]
    rel_a = rel.astype(BF16).astype(F32)
    rel_b = (rel - rel_a).astype(BF16).astype(F32)
    rel_c = rel - rel_a - rel_b
    axial_hot = iota((SEG, 256), 0) == ax
    weighted = jnp.concatenate(
        [jnp.where(axial_hot, part, 0.0).astype(BF16) for part in (rel_a, rel_b, rel_c)], axis=0
    )

    @pl.loop(0, CH)
    def _(h):
        hot = (iota((BW, 256), 0) + h * BW == hw).astype(BF16)
        total = dot_nt(hot, weighted)
        FS[h] = total[:, 0:SEG] + total[:, SEG:2 * SEG] + total[:, 2 * SEG:3 * SEG]

    load_vel().wait()

    burn = rat[0] * 2.0
    h_wall = rat[1] * 2.0
    gain_rate = rat[2] * h_wall
    evap = rat[6] * 4.0
    latent = rat[7] * 4.0

    def gas_slot(s, f, after, last):
        s1 = s + 1
        d = dif[f]
        react = yld[f] * burn * FIELD_SIGN[f]

        def band(h):
            q = S[s, f, h + 1, mid, :]
            ends = E[f, h]
            before = pltpu.roll(jnp.where(lane64 == SEG - 1, ends, q), 1, 1)
            beyond = pltpu.roll(jnp.where(lane64 == 0, ends, q), SEG - 1, 1)
            around = (
                S[s, f, h + 2, mid, :] + S[s, f, h, mid, :]
                + S[s, f, h + 1, 9:73, :] + S[s, f, h + 1, 7:71, :]
                + beyond + before
            )
            fuel = q if f == 2 else S[s, 2, h + 1, mid, :]
            new = q - V[h] * (q - before) + d * (around - 6.0 * q) + react * fuel
            if f == 2:
                new = new + FS[h]
            if f == 0:
                new = new - WM[h]
            if last:
                out_gas[f, h] = new
            else:
                S[s1, f, h + 1, mid, :] = new

        y_pair(s, f, "wait_recv")
        band(0)
        band(CH - 1)
        if not last:
            y_pair(s1, f, "start")
        if after is not None:
            x_pair(s, after, "wait_recv")
            open_band(jnp.where(odd, GR[s, after], GL[s, after]), E.at[after])
        for h in range(1, CH - 1):
            band(h)
        if not last:
            pack_band(s1, f)
            x_pair(s1, f, "start")

    def wall_fluxes(s):
        tl_group(s, "wait_recv")
        for h in range(CH):
            TGC[h:h + 1, :] = S[s, 0, h + 1, 8:9, :]
            TGC[CH + h:CH + h + 1, :] = S[s, 0, h + 1, 71:72, :]

        def side_walls(seen):
            sides = h_wall * (NM[0:16, :] * TGC[0:16, :] - seen)
            for h in range(CH):
                WM[h, 0:1, :] = sides[h:h + 1]
                WM[h, BW - 1:BW, :] = sides[CH + h:CH + h + 1]

        @pl.when(is_end | (s == 0))
        def _():
            seen = pick(CM[...], TL[s])

            @pl.when(is_end)
            def _():
                WM[edge_row - 1] = h_wall * (NM[16:ROWS, :] * S[s, 0, edge_row, mid, :] - seen[16:ROWS])

            side_walls(seen[0:16])

        @pl.when(jnp.logical_not(is_end | (s == 0)))
        def _():
            seen = jnp.zeros((16, SEG), F32)
            for b in range(NC):
                rows = TLR[s, 8 * b:8 * b + 8, :]
                seen = seen + MSK[b] * jnp.concatenate([rows, rows], axis=0)
            side_walls(seen)

    def lining_tables():
        tb_group("wait_recv")
        r = iota((8 * NC, SEG), 0)
        k = (iota((ARC, SEG), 0) + c * ARC).astype(F32)

        def add(b, totals):
            heat, placed, count = totals
            here = r // 8 == b
            low = jnp.where(here, r % 8 * BW, -2).astype(F32)
            high = jnp.where(here, r % 8 * BW + BW - 1, -2).astype(F32)
            rows = ((low == TB[b, 0:1, :]) | (high == TB[b, 0:1, :])).astype(BF16)
            mine = (k == TB[b, 1:2, :]).astype(F32)
            hot = mine.astype(BF16)
            inner = (b > 0) & (b < NC - 1)
            heat = heat + jnp.where(inner, dot_nt(hot, rows), 0.0)
            placed = placed + dot_nt(rows, hot)
            return heat, placed, count + jnp.sum(mine, axis=1, keepdims=True)

        heat, placed, count = lax.fori_loop(
            0, NC, add,
            (jnp.zeros((ARC, 8 * NC), F32), jnp.zeros((8 * NC, ARC), F32), jnp.zeros((ARC, 1), F32)),
        )
        HM[...] = heat.astype(BF16)
        PT[...] = placed.astype(BF16)
        NK[...] = jnp.broadcast_to(count, (ARC, SEG))

    def lining_slot(s, last):
        s1 = s + 1
        if not last:
            pl.when(s == 0)(lining_tables)
        tg_group(s, "wait_recv")
        l_pair(s, "wait_recv")
        c_pair(s, "wait_recv")
        heat = pick(HM[...], TGM[s]) + TGE[s, 0] + TGE[s, 1]
        gain = gain_rate * (heat - NK[...] * L[s, 0, pl.ds(8, ARC), :])
        heat_now = L[s, 0:LD, pl.ds(8, ARC), :]
        soft = jnp.maximum(heat_now, 0.0) + jnp.log1p(jnp.exp(-jnp.abs(heat_now)))
        SE[...] = evap * L[s, LD:2 * LD, pl.ds(8, ARC), :] * soft
        for f in range(3):
            open_arc(jnp.where(odd, LR[s, f], LL[s, f]), f)
        for b in range(NBLK):
            L[s, b, 7:8, :] = HD[s, b:b + 1, :]
            L[s, b, 40:41, :] = HU[s, b:b + 1, :]

        def diffused(f, i):
            deep = min(i + 1, LD - 1)
            shallow = max(i - 1, 0)
            b = f * LD + i
            q = L[s, b, pl.ds(8, ARC), :]
            ends = EL[b]
            before = pltpu.roll(jnp.where(lane32 == SEG - 1, ends, q), 1, 1)
            after = pltpu.roll(jnp.where(lane32 == 0, ends, q), SEG - 1, 1)
            around = (
                L[s, f * LD + deep, pl.ds(8, ARC), :] + L[s, f * LD + shallow, pl.ds(8, ARC), :]
                + L[s, b, 9:41, :] + L[s, b, 7:39, :] + after + before
            )
            return q + rat[3 + f] * (around - 6.0 * q)

        def settle(b, value):
            if last:
                out_lin[b] = value
            else:
                L[s1, b, pl.ds(8, ARC), :] = value

        settle(0, diffused(0, 0) - latent * SE[0] + gain)
        if not last:
            own_surface(s1)
            TLP[s1] = pick(PT[...], L[s1, 0, pl.ds(8, ARC), :])
            TLR[s1, eight_of(c), :] = TLP[s1, eight_of(c), :]
            tl_group(s1, "start")

        for i in range(LD):
            e = SE[i]
            if i > 0:
                settle(i, diffused(0, i) - latent * e)
            settle(LD + i, diffused(1, i) - e)
            settle(2 * LD + i, diffused(2, i) + e)

        if not last:
            lining_margins(s1)
            for f in range(3):
                pack_arc(s1, f)
            c_pair(s1, "start")
            l_pair(s1, "start")

    def substep(s, last):
        first = ORDER[0]
        x_pair(s, first, "wait_recv")
        open_band(jnp.where(odd, GR[s, first], GL[s, first]), E.at[first])
        for f, after in zip(ORDER[:4], ORDER[1:]):
            gas_slot(s, f, after, last)
        wall_fluxes(s)
        gas_slot(s, ORDER[4], None, last)
        if not last:
            own_walls(s + 1)
            tg_group(s + 1, "start")
        lining_slot(s, last)

    @pl.loop(0, SUBSTEPS - 1)
    def _(s):
        substep(s, False)

    substep(SUBSTEPS - 1, True)

    tb_group("wait_send")

    @pl.loop(0, SUBSTEPS)
    def _(s):
        for f in range(NF):
            x_pair(s, f, "wait_send")
            y_pair(s, f, "wait_send")
        l_pair(s, "wait_send")
        c_pair(s, "wait_send")
        tl_group(s, "wait_send")
        tg_group(s, "wait_send")


def leave(gas, lin, shape):
    def body(gas_ref, lin_ref, out_gas, out_lin, sems):
        copies = [
            pltpu.make_async_copy(gas_ref, out_gas, sems.at[0]),
            pltpu.make_async_copy(lin_ref, out_lin, sems.at[1]),
        ]
        for copy in copies:
            copy.start()
        for copy in copies:
            copy.wait()

    out_gas, out_lin = pl.pallas_call(
        body,
        out_shape=(jax.ShapeDtypeStruct(gas.shape, F32), jax.ShapeDtypeStruct(lin.shape, F32)),
        in_specs=[pl.BlockSpec(memory_space=pl.ANY)] * 2,
        out_specs=(pl.BlockSpec(memory_space=pltpu.HBM),) * 2,
        scratch_shapes=[pltpu.SemaphoreType.DMA((2,))],
        compiler_params=pltpu.CompilerParams(vmem_limit_bytes=4 * 1024 * 1024),
    )(gas, lin)
    return out_gas, out_lin.reshape(shape)


def on_device(gas, lining, velocity, diffusion, yields, rates, fire_cells, release, face_cells, face_cycle, face_count):
    lin = lining.reshape(NBLK, ARC, SEG)
    any_ = pl.BlockSpec(memory_space=pl.ANY)
    hbm = pl.BlockSpec(memory_space=pltpu.HBM)
    dma = pltpu.SemaphoreType.DMA
    n = SUBSTEPS
    out_gas, out_lin = pl.pallas_call(
        kernel,
        out_shape=(
            pltpu.VMEM((NF, CH, BW, SEG), F32),
            pltpu.VMEM((NBLK, ARC, SEG), F32),
        ),
        in_specs=[hbm] * 11,
        out_specs=(pl.BlockSpec(memory_space=pltpu.VMEM),) * 2,
        scratch_shapes=[
            pltpu.VMEM((n, NF, CH + 2, 80, SEG), F32),
            pltpu.VMEM((n, NBLK, 48, SEG), F32),
            pltpu.VMEM((CH, BW, SEG), F32),
            pltpu.VMEM((CH, BW, SEG), F32),
            pltpu.VMEM((CH, BW, SEG), F32),
            pltpu.VMEM((n, NF, 8, SEG), F32),
            pltpu.VMEM((n, NF, 8, SEG), F32),
            pltpu.VMEM((n, NF, 8, SEG), F32),
            pltpu.VMEM((n, 3, 8, SEG), F32),
            pltpu.VMEM((n, 3, 8, SEG), F32),
            pltpu.VMEM((n, 3, 8, SEG), F32),
            pltpu.VMEM((n, NBLK, SEG), F32),
            pltpu.VMEM((n, NBLK, SEG), F32),
            pltpu.VMEM((n, NBLK, SEG), F32),
            pltpu.VMEM((n, NBLK, SEG), F32),
            pltpu.VMEM((n, 256, SEG), F32),
            pltpu.VMEM((NC, 8, SEG), F32),
            pltpu.VMEM((ROWS, 256), BF16),
            pltpu.VMEM((256, ROWS), BF16),
            pltpu.VMEM((ROWS, SEG), F32),
            pltpu.VMEM((ARC, 8 * NC), BF16),
            pltpu.VMEM((8 * NC, ARC), BF16),
            pltpu.VMEM((ARC, SEG), F32),
            pltpu.VMEM((NC, 16, SEG), F32),
            pltpu.VMEM((n, 8 * NC, SEG), F32),
            pltpu.VMEM((n, 8 * NC, SEG), F32),
            pltpu.VMEM((ROWS, SEG), F32),
            pltpu.VMEM((n, 8 * NC, SEG), F32),
            pltpu.VMEM((n, 256, SEG), F32),
            pltpu.VMEM((n, 8 * NC, SEG), F32),
            pltpu.VMEM((n, 2, ARC, SEG), F32),
            pltpu.VMEM((NF, CH, BW, SEG), F32),
            pltpu.VMEM((NBLK, ARC, SEG), F32),
            pltpu.VMEM((LD, ARC, SEG), F32),
            pltpu.SMEM((NF,), F32),
            pltpu.SMEM((NF,), F32),
            pltpu.SMEM((8,), F32),
            pltpu.SMEM((1,), jnp.int32),
            pltpu.VMEM((1, 256), jnp.int32),
            pltpu.VMEM((1, 256), F32),
            pltpu.VMEM((1, ROWS), jnp.int32),
            pltpu.VMEM((1, ROWS), jnp.int32),
            dma((n, NF, 2)), dma((n, NF, 2)),
            dma((n, NF, 2)), dma((n, NF, 2)),
            dma((n, 2)), dma((n, 2)),
            dma((n, 2)), dma((n, 2)),
            dma((n, NC - 1)), dma((n, NC - 1)),
            dma((n, NC - 1)), dma((n, NC - 1)),
            dma((NC - 1,)), dma((NC - 1,)),
            dma((15,)),
        ],
        compiler_params=pltpu.CompilerParams(
            collective_id=0, has_side_effects=True, vmem_limit_bytes=56 * 1024 * 1024
        ),
    )(
        gas, lin, velocity, diffusion, yields, rates,
        fire_cells.reshape(1, -1), release.reshape(1, -1),
        face_cells.reshape(1, -1), face_cycle.reshape(1, -1), face_count,
    )
    return leave(out_gas, out_lin, lining.shape)


def solution(mesh):
    in_specs = (
        P(None, "cross", None, "tunnel"),
        P(None, None, "cross", "tunnel"),
        P("cross", None, "tunnel"),
        P(), P(), P(), P(), P(),
        P(("tunnel", "cross")),
        P(("tunnel", "cross")),
        P(("tunnel", "cross")),
    )
    out_specs = (P(None, "cross", None, "tunnel"), P(None, None, "cross", "tunnel"))
    return jax.shard_map(on_device, mesh=mesh, in_specs=in_specs, out_specs=out_specs, check_vma=False)
```

profile of v0, /device:TPU:4, one launch (start us, length us, event | category | flops | bytes accessed | tf_op | source)
XLA Modules:
  0.0 40.1 jit_solution(16439008223330512613)
XLA Ops:
  1.3 37.5 %shard_map.122 = (f32[5,8,64,128]{3,2,1,0:T(8,128)S(1)}, f32[48,32,128]{2,1,0:T(8,128)S(1)}) custom-call(f32[5,8,64,128]{3,2,1,0:T(8,128)} %gas.1, f32[48,32,128]{2,1,0:T(8,128)} %bitcast.6, f32[8,64,128]{2,1,0:T(8,128)} %vel.1, f32[5]{0:T(128)} %dif_in.1, f32[5]{0:T(128)} %yld_in.1, f32[8]{0:T(128)} %rat_in.1, s32[1,256]{1,0:T(1,128)} %bitcast.7, ...), custom_call_target="tpu_custom_call" | custom-call | tf_op jit(solution)/shard_map/pallas_call | solution.py:614
  38.8 1.3 %shard_map.123 = (f32[5,8,64,128]{3,2,1,0:T(8,128)}, f32[48,32,128]{2,1,0:T(8,128)}) custom-call(f32[5,8,64,128]{3,2,1,0:T(8,128)S(1)} %get-tuple-element.6.gas_ref, f32[48,32,128]{2,1,0:T(8,128)S(1)} %get-tuple-element.7.lin_ref), custom_call_target="tpu_custom_call" | custom-call | tf_op jit(solution)/shard_map/pallas_call | solution.py:597
where the time goes:
time: 40.2 us; the launch traced here: 40.1 us
  Pallas kernels  38.8 us (97%)
  between operations  1.29 us (3%)
    pallas_call x1, Pallas kernels, on_device(): pl.pallas_call(kernel, out_shape=(pltpu.VMEM((NF, CH, BW, SEG), F32), plt...  37.5 us
    pallas_call x1, Pallas kernels, leave(): pl.pallas_call(body, out_shape=(jax.ShapeDtypeStruct(gas.shape, F32), jax...  1.33 us

commit v1 on v0

--- a/solution.py
+++ b/solution.py
@@ -422,17 +422,16 @@
             else:
                 S[s1, f, h + 1, mid, :] = new
 
+        if after is not None:
+            x_pair(s, after, "wait_recv")
+            open_band(jnp.where(odd, GR[s, after], GL[s, after]), E.at[after])
+        for h in range(1, CH - 1):
+            band(h)
         y_pair(s, f, "wait_recv")
         band(0)
         band(CH - 1)
         if not last:
             y_pair(s1, f, "start")
-        if after is not None:
-            x_pair(s, after, "wait_recv")
-            open_band(jnp.where(odd, GR[s, after], GL[s, after]), E.at[after])
-        for h in range(1, CH - 1):
-            band(h)
-        if not last:
             pack_band(s1, f)
             x_pair(s1, f, "start")
 
@@ -536,6 +535,7 @@
             TLP[s1] = pick(PT[...], L[s1, 0, pl.ds(8, ARC), :])
             TLR[s1, eight_of(c), :] = TLP[s1, eight_of(c), :]
             tl_group(s1, "start")
+            tg_group(s1, "start")
 
         for i in range(LD):
             e = SE[i]
@@ -561,7 +561,6 @@
         gas_slot(s, ORDER[4], None, last)
         if not last:
             own_walls(s + 1)
-            tg_group(s + 1, "start")
         lining_slot(s, last)
 
     @pl.loop(0, SUBSTEPS - 1)

time: 40.2 us -> 39.8 us (0.990)
  Pallas kernels: 38.8 us -> 38.3 us
    pallas_call x1, Pallas kernels: 37.5 us -> 37 us  [on_device(): pl.pallas_call(kernel, out_shape=(pltpu.VMEM((NF, CH, BW, SEG), F32), plt...]
where the time goes in v1:
time: 39.8 us; the launch traced here: 39.6 us
  Pallas kernels  38.3 us (96%)
  between operations  1.29 us (3%)
    pallas_call x1, Pallas kernels, on_device(): pl.pallas_call(kernel, out_shape=(pltpu.VMEM((NF, CH, BW, SEG), F32), plt...  37 us
    pallas_call x1, Pallas kernels, leave(): pl.pallas_call(body, out_shape=(jax.ShapeDtypeStruct(gas.shape, F32), jax...  1.33 us

profile of v1, /device:TPU:4, one launch (start us, length us, event | category | flops | bytes accessed | tf_op | source)
XLA Modules:
  0.0 39.6 jit_solution(15546370744785741828)
XLA Ops:
  1.3 37.0 %shard_map.122 = (f32[5,8,64,128]{3,2,1,0:T(8,128)S(1)}, f32[48,32,128]{2,1,0:T(8,128)S(1)}) custom-call(f32[5,8,64,128]{3,2,1,0:T(8,128)} %gas.1, f32[48,32,128]{2,1,0:T(8,128)} %bitcast.6, f32[8,64,128]{2,1,0:T(8,128)} %vel.1, f32[5]{0:T(128)} %dif_in.1, f32[5]{0:T(128)} %yld_in.1, f32[8]{0:T(128)} %rat_in.1, s32[1,256]{1,0:T(1,128)} %bitcast.7, ...), custom_call_target="tpu_custom_call" | custom-call | tf_op jit(solution)/shard_map/pallas_call | solution.py:613
  38.3 1.3 %shard_map.123 = (f32[5,8,64,128]{3,2,1,0:T(8,128)}, f32[48,32,128]{2,1,0:T(8,128)}) custom-call(f32[5,8,64,128]{3,2,1,0:T(8,128)S(1)} %get-tuple-element.6.gas_ref, f32[48,32,128]{2,1,0:T(8,128)S(1)} %get-tuple-element.7.lin_ref), custom_call_target="tpu_custom_call" | custom-call | tf_op jit(solution)/shard_map/pallas_call | solution.py:596
